TPU v7x, 32 devices: a whole 2x2x4 slice. The times are simulated.
32 devices in a mesh: morton: 8 (over z, x), slab: 4 (over y, core).
Axes of the slice: x: 2, y: 2, z: 4, core: 2. Of those that a mesh axis runs over, the one named last changes fastest.
Arguments:
- multipole: bfloat16 [3, 488, 8192], P(None, None, ('morton', 'slab')), may hold values from -1.796875 to 1.796875
- positions: bfloat16 [3, 128, 8192], P(None, None, ('morton', 'slab')), may hold values from 0 to 1
- strengths: bfloat16 [3, 128, 8192], P(None, None, ('morton', 'slab')), may hold values from -3 to 3
- vlist: int32 [27, 8192], P(None, ('morton', 'slab')), may hold values from -1 to 48, as said below
- ulist: int32 [9, 8192], P(None, ('morton', 'slab')), may hold values from -1 to 8, as said below
Outputs:
- check: float32 [3, 488, 8192], P(None, None, ('morton', 'slab'))
- potential: float32 [3, 128, 8192], P(None, None, ('morton', 'slab'))
Inputs may be any that keep to these rules, and one draw needn't show every extreme that they name: `vlist`: entry k of leaf t is -1 or the code 7 * (dx + 3) + (dy + 3) of the k-th offset, in increasing code, of the leaf's pattern: the offsets with dx from -2 - (x_t % 2) to 3 - (x_t % 2) and dy from -2 - (y_t % 2) to 3 - (y_t % 2), except those with |dx| <= 1 and |dy| <= 1. It is -1 exactly where the leaf (x_t + dx, y_t + dy) lies outside the grid or one of the two leaves is unoccupied; occupancy is the same as in ulist. `ulist`: entry k of leaf t is -1 or k, naming the offset dx = k // 3 - 1, dy = k % 3 - 1; it is -1 exactly where that leaf lies outside the grid or one of the two leaves is unoccupied.
All inputs are finite; a program needn't handle non-finite values.
Results may differ from a plain program's by a relative error of at most 0.003.
Values may be sent and summed in bfloat16 or wider, within the bound.
A program may use at most 128 MiB of HBM per device.

v0:
```python
from functools import partial
import math

import jax
import jax.numpy as jnp
import numpy as np
from jax import lax
from jax.sharding import PartitionSpec as P

SIDE = 16
EQ_SIDE = 10


FOUR_PI = 4.0 * math.pi
DELTA_SQ = 0.01
RADIUS = 0.525


def from_behind(value, axis, steps):
    count = lax.axis_size(axis)
    leading, last = (max(0, -steps), min(count, count - steps))
    return lax.ppermute(value, axis, [(source, source + steps) for source in range(leading, last)])


def surface_points(per_edge):
    grid_line = np.linspace(-1.0, 1.0, per_edge)
    first, second, third = np.meshgrid(grid_line, grid_line, grid_line, indexing="ij")
    stacked = np.stack([first.ravel(), second.ravel(), third.ravel()], axis=1)
    on_face = np.max(np.abs(stacked), axis=1) > 0.999
    return (stacked[on_face] * RADIUS).astype(np.float32)


def class_offsets(parity_x, parity_y):
    listed = []
    for shift_x in range(-2 - parity_x, 4 - parity_x):
        for shift_y in range(-2 - parity_y, 4 - parity_y):
            if abs(shift_x) > 1 or abs(shift_y) > 1:
                listed.append((shift_x, shift_y))
    return listed


def translation(shift_x, shift_y):
    points = jnp.asarray(surface_points(EQ_SIDE))
    delta_x = points[:, None, 0] - points[None, :, 0] - shift_x
    delta_y = points[:, None, 1] - points[None, :, 1] - shift_y
    delta_z = points[:, None, 2] - points[None, :, 2]
    distance = jnp.sqrt(delta_x * delta_x + delta_y * delta_y + delta_z * delta_z)
    return (1.0 / (FOUR_PI * distance)).astype(jnp.bfloat16)


def join_quadrants(quads):
    lower = jnp.concatenate([quads[0], quads[1]], axis=-1)
    upper = jnp.concatenate([quads[2], quads[3]], axis=-1)
    return jnp.concatenate([lower, upper], axis=-2)


def cut_window(wide, margin, quad_x, quad_y):
    rows_cut = lax.dynamic_slice_in_dim(wide, quad_y * SIDE, SIDE + 2 * margin, 2)
    return lax.dynamic_slice_in_dim(rows_cut, quad_x * SIDE, SIDE + 2 * margin, 3)


def whole_tile(multi_grid, particle_grid, quad_x, quad_y):
    quads_multi, quads_particle = (
        lax.all_gather(multi_grid[None], "slab", axis=0, tiled=True),
        lax.all_gather(particle_grid[None], "slab", axis=0, tiled=True),
    )
    tile_multi = join_quadrants(quads_multi)
    tile_particle = join_quadrants(quads_particle)
    west = from_behind((tile_multi[..., -3:], tile_particle[..., -1:]), "morton", 1)
    east = from_behind((tile_multi[..., :3], tile_particle[..., :1]), "morton", -1)
    wide_multi = jnp.concatenate([west[0], tile_multi, east[0]], axis=-1)
    wide_particle = jnp.concatenate([west[1], tile_particle, east[1]], axis=-1)
    wide_multi = jnp.pad(wide_multi, ((0, 0), (0, 0), (3, 3), (0, 0)))
    wide_particle = jnp.pad(wide_particle, ((0, 0), (0, 0), (1, 1), (0, 0)))
    return (cut_window(wide_multi, 3, quad_x, quad_y), cut_window(wide_particle, 1, quad_x, quad_y))


def far_field(multi_full, lists):
    eq_count = multi_full.shape[1]
    half_side = SIDE // 2
    result = jnp.zeros((3, eq_count, SIDE, SIDE), jnp.float32)
    for parity_y in (0, 1):
        for parity_x in (0, 1):
            partial_sum = jnp.zeros((3, eq_count, half_side, half_side), jnp.float32)
            for entry, (shift_x, shift_y) in enumerate(class_offsets(parity_x, parity_y)):
                top = 3 + parity_y + shift_y
                left = 3 + parity_x + shift_x
                source = lax.slice(
                    multi_full,
                    (0, 0, top, left),
                    (3, eq_count, top + SIDE - 1, left + SIDE - 1),
                    (1, 1, 2, 2),
                )
                live_mask = (lists[entry, parity_y::2, parity_x::2] >= 0).astype(jnp.bfloat16)
                partial_sum = partial_sum + jnp.einsum(
                    "ij,cjab->ciab",
                    translation(shift_x, shift_y),
                    source * live_mask,
                    preferred_element_type=jnp.float32,
                )
            result = result.at[:, :, parity_y::2, parity_x::2].set(partial_sum)
    return result.reshape(3, eq_count, SIDE * SIDE)


def row_potential(place, weight, lists, width, leaf_row):
    target = lax.dynamic_slice_in_dim(place, leaf_row + 1, 1, 2)[:, :, 0, 1 : width + 1].transpose(
        0, 2, 1
    )
    summed = jnp.zeros(target.shape, jnp.float32)
    for shift_x in (-1, 0, 1):
        for shift_y in (-1, 0, 1):
            entry = (shift_x + 1) * 3 + shift_y + 1
            source = lax.dynamic_slice_in_dim(place, leaf_row + 1 + shift_y, 1, 2)[
                :, :, 0, 1 + shift_x : 1 + shift_x + width
            ].transpose(0, 2, 1)
            charge = lax.dynamic_slice_in_dim(weight, leaf_row + 1 + shift_y, 1, 2)[
                :, :, 0, 1 + shift_x : 1 + shift_x + width
            ].transpose(0, 2, 1)
            present = (lax.dynamic_slice_in_dim(lists[entry], leaf_row, 1, 0)[0] >= 0).astype(
                jnp.float32
            )
            delta_x = target[0][:, :, None] - (source[0][:, None, :] + shift_x)
            delta_y = target[1][:, :, None] - (source[1][:, None, :] + shift_y)
            delta_z = target[2][:, :, None] - source[2][:, None, :]
            squared = delta_x * delta_x + delta_y * delta_y + delta_z * delta_z
            kernel_row = present[:, None, None] / (FOUR_PI * jnp.sqrt(squared + DELTA_SQ))
            summed = summed + jnp.sum(kernel_row[None] * charge[:, :, None, :], axis=-1)
    return summed


def near_field(particle_full, lists):
    per_leaf = particle_full.shape[1]
    place = particle_full[:3].astype(jnp.float32)
    weight = particle_full[3:].astype(jnp.float32)
    rows = lax.map(
        partial(row_potential, place, weight, lists, SIDE), jnp.arange(SIDE, dtype=jnp.int32)
    )
    return rows.transpose(1, 3, 0, 2).reshape(3, per_leaf, SIDE * SIDE)


def body(multipole, positions, strengths, vlist, ulist):
    eq_count = multipole.shape[1]
    per_leaf = positions.shape[1]
    slab_index = lax.axis_index("slab")
    quad_x = slab_index % 2
    quad_y = slab_index // 2
    multi_grid = multipole.reshape(3, eq_count, SIDE, SIDE)
    particle_grid = jnp.concatenate([positions, strengths], axis=0).reshape(6, per_leaf, SIDE, SIDE)
    multi_full, particle_full = whole_tile(multi_grid, particle_grid, quad_x, quad_y)
    check = far_field(multi_full, vlist.reshape(27, SIDE, SIDE))
    potential = near_field(particle_full, ulist.reshape(9, SIDE, SIDE))
    return (check, potential)


def solution(mesh):
    in_specs = (
        P(None, None, ("morton", "slab")),
        P(None, None, ("morton", "slab")),
        P(None, None, ("morton", "slab")),
        P(None, ("morton", "slab")),
        P(None, ("morton", "slab")),
    )
    out_specs = (P(None, None, ("morton", "slab")), P(None, None, ("morton", "slab")))
    return jax.shard_map(body, mesh=mesh, in_specs=in_specs, out_specs=out_specs, check_vma=False)
```

profile of v0, /device:TPU:3, one launch (start us, length us, event | category | flops | bytes accessed | tf_op | source)
XLA Modules:
  0.0 778.8 jit_solution(6151055700652776252)
XLA Ops:
  46.5 3.4 iota_compare_fusion
  51.7 3.2 collective-permute-start.2
  61.2 3.3 fusion.402
  75.6 381.7 %while.14 = (s32[]{:T(128)}, f32[16,3,16,128]{3,2,0,1:T(8,128)}, s32[9,16,16]{2,1,0:T(8,128)S(1)}, s32[16]{0:T(128)}, f32[3,128,18,18]{1,3,0,2:T(8,128)S(1)}, /*...) while((s32[]{:T(128)}, f32[16,3,16,128]{3,2,0,1:T(8,128)}, ...), condition=%wide.region_14.15_spmd, body=%wide.region_4.14_spmd.sunk | while | flops 40126768 | bytes 21180976 | solution.py:135
  89.7 3.1 multiply_divide_fusion.12
  112.8 3.1 multiply_divide_fusion.12
  459.2 8.0 %fusion.36 = bf16[3,488,22,22]{1,3,2,0:T(8,128)(2,1)S(1)} fusion(s32[]{:T(128)S(6)} %select_n.93, s32[]{:T(128)S(6)} %select_n.96, bf16[3,488,16,16]{1,3,2,0:T(8,128)(2,1)} %copy-done.1, bf16[3,488,16,16]{1,3,2,0:T(8,128)(2,1)} %copy-done, bf16[3,488,16,16]{1,3,2,0:T(8,128)(2,1)S(1)} %get-tuple-element.235, ...), kind=kLoop, calls=%fused_computation.154 | loop fusion | flops 16297248 | bytes 6396288 | tf_op jit(solution)/shard_map/concatenate | solution.py:71
  467.9 7.5 slice.2384
  475.4 7.4 slice.2379
  482.8 7.4 slice.2374
  490.9 7.5 slice.2399
  498.3 7.4 slice.2414
  505.8 7.4 slice.2369
  513.2 7.4 slice.2653
  520.6 7.4 slice.2409
  528.0 7.4 slice.2640
  535.5 7.4 slice.2394
  542.9 7.4 slice.2389
  550.4 7.5 slice.2527
  557.8 7.4 slice.2522
  565.2 7.4 slice.2517
  574.3 7.5 slice.2479
  581.8 7.4 slice.2474
  589.2 7.5 slice.2469
  596.7 7.4 slice.2464
  605.8 7.5 slice.2434
  613.3 7.4 slice.2429
  620.7 7.4 slice.2424
  630.6 7.5 slice.2419
  638.1 7.5 slice.2404
  753.2 5.2 scatter_fusion
  758.4 5.2 scatter_fusion.1
  (1026 shorter events, 449.5 us)
Async XLA Ops:
  7.2 4.4 copy-start.30
  7.2 42.7 %all-gather.5.cloned.1.call-start = ((), (), s32[]{:S(2)}) async-start(), calls=%async_computation.1 | async-start | bytes 1966080 | tf_op jit(solution)/shard_map/all_gather | solution.py:65
  9.2 55.4 %all-gather.3.cloned.1.call-start = ((), (), s32[]{:S(2)}) async-start(), calls=%async_computation | async-start | bytes 3932160 | tf_op jit(solution)/shard_map/all_gather | solution.py:64
  49.9 10.2 %copy-start.31 = (s32[9,256]{1,0:T(8,128)S(1)}, s32[9,256]{1,0:T(8,128)}, u32[]{:S(2)}) copy-start(s32[9,256]{1,0:T(8,128)} %param.119) | copy-start | bytes 27652
  51.7 8.4 %collective-permute-start.2 = (bf16[6,128,32,1]{1,3,2,0:T(2,128)(2,1)S(1)}, bf16[6,128,32,1]{1,3,2,0:T(2,128)(2,1)S(1)}, u32[]{:S(2)}, u32[]{:S(2)}) collective-permute-start(bf16[6,128,32,1]{1,3,2,0:T(2,128)(2,1)S(1)} %get-tuple-element.239), channel_id=1, source_target_pairs={{0,4},{4,8},{8,12},{12,16},{16,20},{20,24},{24,28},{1,5},{5,9},{9,... | collective-permute-start | bytes 147464 | tf_op jit(solution)/shard_map/ppermute | solution.py:22
  54.9 6.3 collective-permute-start.3
  66.9 2.1 copy-start.1
  69.0 390.2 %collective-permute-start = (bf16[3,488,32,3]{1,3,2,0:T(4,128)(2,1)}, bf16[3,488,32,3]{1,3,2,0:T(4,128)(2,1)}, u32[]{:S(2)}, u32[]{:S(2)}) collective-permute-start(bf16[3,488,32,3]{1,3,2,0:T(4,128)(2,1)} %get-tuple-element.233), channel_id=1, source_target_pairs={{0,4},{4,8},{8,12},{12,16},{16,20},{20,24},{24,28},{1,5},{5,9},{9,... | collective-permute-start | bytes 843272 | tf_op jit(solution)/shard_map/ppermute | solution.py:22
  72.1 387.1 %collective-permute-start.1 = (bf16[3,488,32,3]{1,3,2,0:T(4,128)(2,1)}, bf16[3,488,32,3]{1,3,2,0:T(4,128)(2,1)}, u32[]{:S(2)}, u32[]{:S(2)}) collective-permute-start(bf16[3,488,32,3]{1,3,2,0:T(4,128)(2,1)} %get-tuple-element.232), channel_id=1, source_target_pairs={{4,0},{8,4},{12,8},{16,12},{20,16},{24,20},{28,24},{5,1},{9,5},{13... | collective-permute-start | bytes 843272 | tf_op jit(solution)/shard_map/ppermute | solution.py:22
  572.7 72.9 %copy-start.86 = (bf16[8,8]{1,0:T(8,128)(2,1)S(1)}, bf16[8,8]{1,0:T(8,128)(2,1)}, u32[]{:S(2)}) copy-start(bf16[8,8]{1,0:T(8,128)(2,1)} %get-tuple-element.332) | copy-start | bytes 388
  572.7 72.9 %copy-start.106 = (f32[488]{0:T(512)S(1)}, f32[488]{0:T(512)}, u32[]{:S(2)}) copy-start(f32[488]{0:T(512)} %constant.409) | copy-start | bytes 5860
  572.7 72.9 %copy-start.107 = (f32[488]{0:T(512)S(1)}, f32[488]{0:T(512)}, u32[]{:S(2)}) copy-start(f32[488]{0:T(512)} %constant.411) | copy-start | bytes 5860
  572.7 72.9 %copy-start.108 = (f32[488]{0:T(512)S(1)}, f32[488]{0:T(512)}, u32[]{:S(2)}) copy-start(f32[488]{0:T(512)} %constant.413) | copy-start | bytes 5860
  572.7 72.9 %copy-start.109 = (f32[488]{0:T(512)S(1)}, f32[488]{0:T(512)}, u32[]{:S(2)}) copy-start(f32[488]{0:T(512)} %constant.414) | copy-start | bytes 5860
  645.6 1.7 copy-start.12
  645.6 1.7 copy-start.92
  645.6 1.7 copy-start.110
  645.6 1.7 copy-start.111
  659.6 1.3 copy-start.25
  659.6 1.3 copy-start.85
  670.3 1.1 copy-start.24
  701.7 1.3 copy-start.66
  722.7 1.1 copy-start.48
  723.8 2.1 copy-start.42
  730.5 1.1 copy-start.64
  744.6 1.2 copy-start.47
  749.5 1.2 copy-start.33
  750.7 2.6 copy-start.5
  751.7 6.7 copy-start.4
  751.7 11.9 %copy-start.3 = (s32[64]{0:T(128)S(1)}, s32[64]{0:T(128)}, u32[]{:S(2)}) copy-start(s32[64]{0:T(128)} %reshape.2152) | copy-start | bytes 772
  751.7 15.0 %copy-start.2 = (s32[64]{0:T(128)S(1)}, s32[64]{0:T(128)}, u32[]{:S(2)}) copy-start(s32[64]{0:T(128)} %reshape.2158) | copy-start | bytes 772
  751.7 15.0 %copy-start.6 = (f32[64,3,488]{2,1,0:T(4,128)S(1)}, f32[64,3,488]{2,1,0:T(4,128)}, u32[]{:S(2)}) copy-start(f32[64,3,488]{2,1,0:T(4,128)} %copy.157) | copy-start | bytes 1124356
  (86 other events, 79.5 us)
Sparse Core Ops, SparseCore 0:
  10.1 21.2 all-gather.4
  33.0 28.6 all-gather.2
where the time goes:
time: 791 us; the launch traced here: 779 us
  other arithmetic  297 us (38%)
  local copies, waits for them, and re-layouts  245 us (31%)
  loops' own time  107 us (14%)
  matrix products  101 us (13%)
  between operations  17.1 us (2%)
  starting transfers between devices  11.4 us (1%)
    slice x32, local copies, waits for them, and re-layouts, far_field(): lax.slice(multi_full, (0, 0, top, left), (3, eq_count, top + SIDE - 1, le...  178 us
    reduce_sum x144, other arithmetic, row_potential(): summed = summed + jnp.sum(kernel_row[None] * charge[:, :, None, :], axis=-1)  128 us
    div x48, other arithmetic, row_potential(): present[:, None, None] / (FOUR_PI * jnp.sqrt(squared + DELTA_SQ))  114 us
    another operation x1, loops' own time, near_field(): lax.map(partial(row_potential, place, weight, lists, SIDE), jnp.arange(SI...  107 us
    dot_general x108, matrix products, far_field(): jnp.einsum('ij,cjab->ciab', translation(shift_x, shift_y), source * live_...  101 us
    convert_element_type x54, other arithmetic, far_field(): (lists[entry, parity_y::2, parity_x::2] >= 0).astype(jnp.bfloat16)  23.8 us
    dynamic_slice x16, local copies, waits for them, and re-layouts, near_field(): lax.map(partial(row_potential, place, weight, lists, SIDE), jnp.arange(SI...  19.9 us
    scatter x4, local copies, waits for them, and re-layouts, far_field(): result = result.at[:, :, parity_y::2, parity_x::2].set(partial_sum)  16.6 us
  transfers between devices with their start and end apart: 6, of which 1 were waited for; matrix products, arithmetic and copies ran while one was open for 42% of the time, Pallas kernels for 0%

commit v1 on v0

v1 whole, which is shorter than its diff:
```python
import math
from functools import partial

import jax
import jax.numpy as jnp
import ml_dtypes
import numpy as np
from jax import lax
from jax.experimental import pallas as pl
from jax.experimental.pallas import tpu as pltpu
from jax.sharding import PartitionSpec as P

SIDE = 16
EQ_SIDE = 10
FOUR_PI = 4.0 * math.pi
DELTA_SQ = 0.01
RADIUS = 0.525
HALF = 256
WIDE = SIDE + 4
BF16 = jnp.bfloat16
F32 = jnp.float32


def surface_points():
    grid_line = np.linspace(-1.0, 1.0, EQ_SIDE)
    first, second, third = np.meshgrid(grid_line, grid_line, grid_line, indexing="ij")
    stacked = np.stack([first.ravel(), second.ravel(), third.ravel()], axis=1)
    on_face = np.max(np.abs(stacked), axis=1) > 0.999
    return (stacked[on_face] * RADIUS).astype(np.float32)


def translation(points, shift_x, shift_y):
    delta = points[:, None, :] - points[None, :, :]
    ex = delta[..., 0] - np.float32(shift_x)
    ey = delta[..., 1] - np.float32(shift_y)
    ez = delta[..., 2]
    distance = np.sqrt(ex * ex + ey * ey + ez * ez)
    table = (np.float32(1.0) / (np.float32(FOUR_PI) * distance)).astype(ml_dtypes.bfloat16)
    return table.astype(np.float32)


def mirror_halves(points):
    upper = np.nonzero(points[:, 2] > 0)[0]
    mirrored = points[upper] * np.array([1.0, 1.0, -1.0], np.float32)
    gap = np.abs(mirrored[:, None, :] - points[None, :, :]).max(-1)
    lower = gap.argmin(1)
    return upper, lower


def class_offsets(parity_x, parity_y):
    listed = []
    for shift_x in range(-2 - parity_x, 4 - parity_x):
        for shift_y in range(-2 - parity_y, 4 - parity_y):
            if abs(shift_x) > 1 or abs(shift_y) > 1:
                listed.append((shift_x, shift_y))
    return listed


def far_tables():
    points = surface_points()
    upper, lower = mirror_halves(points)
    half, count = len(upper), len(points)
    offsets = [(x, y) for x in range(-3, 4) for y in range(-3, 4) if max(abs(x), abs(y)) > 1]
    weights = np.zeros((len(offsets), 2, HALF, HALF), ml_dtypes.bfloat16)
    for n, (x, y) in enumerate(offsets):
        table = translation(points, x, y)
        same = table[np.ix_(upper, upper)]
        cross = table[np.ix_(upper, lower)]
        weights[n, 0, :half, :half] = (same + cross).T
        weights[n, 1, :half, :half] = (same - cross).T
    fold = np.zeros((count, 2 * HALF), np.float32)
    cols = np.arange(half)
    fold[upper, cols] = 1
    fold[lower, cols] = 1
    fold[upper, HALF + cols] = 1
    fold[lower, HALF + cols] = -1
    unfold = np.concatenate([fold, fold], axis=1) * 0.5
    steps = []
    for n, (x, y) in enumerate(offsets):
        for parity_y in (0, 1):
            for parity_x in (0, 1):
                if (x, y) in class_offsets(parity_x, parity_y):
                    start_x, start_y = 2 + parity_x + x, 2 + parity_y + y
                    steps.append(
                        (n, start_x * 2 + start_y % 2, start_y // 2, parity_y * 2 + parity_x)
                    )
    steps = np.array(steps, np.int32)
    return weights, fold.astype(ml_dtypes.bfloat16), unfold.astype(ml_dtypes.bfloat16), steps


def far_kernel(steps, windows, weights, out, acc):
    acc[...] = jnp.zeros_like(acc)

    def step(n, carry):
        table, window, row, leaf_class = steps[n, 0], steps[n, 1], steps[n, 2], steps[n, 3]
        for e in range(2):
            cols = slice(e * HALF, (e + 1) * HALF)
            source = windows[window, pl.ds(row, 8), :, cols].reshape(256, HALF)
            acc[leaf_class, :, cols] += jnp.dot(
                source, weights[table, e], preferred_element_type=F32
            )
        return carry

    lax.fori_loop(0, steps.shape[0], step, 0, unroll=2)

    def finish(n, carry):
        value = acc[n]
        high = value.astype(BF16)
        out[n, :, : 2 * HALF] = high
        out[n, :, 2 * HALF :] = (value - high.astype(F32)).astype(BF16)
        return carry

    lax.fori_loop(0, 4, finish, 0)


def far_field(windows, weights, steps):
    return pl.pallas_call(
        far_kernel,
        out_shape=jax.ShapeDtypeStruct((4, 256, 4 * HALF), BF16),
        in_specs=[
            pl.BlockSpec(memory_space=pltpu.SMEM),
            pl.BlockSpec(memory_space=pltpu.VMEM),
            pl.BlockSpec(memory_space=pltpu.VMEM),
        ],
        out_specs=pl.BlockSpec(memory_space=pltpu.VMEM),
        scratch_shapes=[pltpu.VMEM((4, 256, 2 * HALF), F32)],
        compiler_params=pltpu.CompilerParams(vmem_limit_bytes=44 * 2**20),
        name="far",
    )(steps, windows, weights)


def near_kernel(target_ref, source_ref, charge_ref, out_ref):
    y = pl.program_id(0)
    leaf = 128
    first_three = lax.broadcasted_iota(jnp.int32, (16, leaf), 0) < 3
    left_half = lax.broadcasted_iota(jnp.int32, (16, 2 * leaf), 1) < leaf
    contract = (((0,), (0,)), ((), ()))

    def pair(i, carry):
        base = pl.multiple_of(i * 2 * leaf, 2 * leaf)
        target = target_ref[y + 1, :, pl.ds(base + leaf, 2 * leaf)]
        nothing = jnp.zeros((16, leaf), BF16)
        split = jnp.concatenate(
            [
                jnp.concatenate([target[:, :leaf], nothing], axis=1),
                jnp.concatenate([nothing, target[:, leaf:]], axis=1),
            ],
            axis=0,
        )
        total = jnp.zeros((16, 2 * leaf), F32)
        for k in range(3):
            source = source_ref[y + k, :, pl.ds(base, 4 * leaf)]
            charge = charge_ref[y + k, :, pl.ds(base, 4 * leaf)]
            middle = lax.dot_general(
                source[:, leaf : 3 * leaf], target, contract, preferred_element_type=F32
            )
            outer = jnp.concatenate([source[:, :leaf], source[:, 3 * leaf :]], axis=0)
            edge = lax.dot_general(outer, split, contract, preferred_element_type=F32)
            total += jnp.dot(
                charge[:, leaf : 3 * leaf],
                lax.rsqrt(middle).astype(BF16),
                preferred_element_type=F32,
            )
            total += jnp.dot(
                jnp.where(first_three, charge[:, :leaf], charge[:, 3 * leaf :]),
                lax.rsqrt(edge).astype(BF16),
                preferred_element_type=F32,
            )
        chosen = jnp.where(left_half, total, pltpu.roll(total, 16 - 3, 0))
        out_ref[0, :, pl.ds(base, 2 * leaf)] = chosen[:8] * (1.0 / FOUR_PI)
        return carry

    lax.fori_loop(0, SIDE // 2, pair, 0, unroll=2)


def near_field(target, source, charge):
    lanes = target.shape[-1]
    whole = pl.BlockSpec((SIDE + 2, 16, lanes), lambda y: (0, 0, 0))
    return pl.pallas_call(
        near_kernel,
        grid=(SIDE,),
        out_shape=jax.ShapeDtypeStruct((SIDE, 8, SIDE * 128), F32),
        in_specs=[whole, whole, whole],
        out_specs=pl.BlockSpec((1, 8, SIDE * 128), lambda y: (y, 0, 0)),
        compiler_params=pltpu.CompilerParams(vmem_limit_bytes=40 * 2**20),
        name="near",
    )(target, source, charge)


def with_halo(square):
    tiles = lax.axis_size("morton")
    quad_y = lax.axis_index("slab") // 2
    sent = jnp.where(quad_y == 0, square[-2:], square[:2])
    other = lax.ppermute(sent, "slab", [(0, 2), (1, 3), (2, 0), (3, 1)])
    blank = jnp.zeros_like(other)
    below = jnp.where(quad_y == 0, blank, other)
    above = jnp.where(quad_y == 0, other, blank)
    tall = jnp.concatenate([below, square, above], axis=0)

    def index(x, y):
        return (x // 2) * 4 + 2 * y + x % 2

    eastward = [(index(x, y), index(x + 1, y)) for x in range(2 * tiles - 1) for y in (0, 1)]
    westward = [(b, a) for a, b in eastward]
    axes = ("morton", "slab")
    west = lax.ppermute(tall[:, -2:], axes, eastward)
    east = lax.ppermute(tall[:, :2], axes, westward)
    return jnp.concatenate([west, tall, east], axis=1)


def near_inputs(places, charges):
    edge = SIDE + 2
    spread = jnp.zeros((edge, edge, 128), F32)
    leaf_x = spread + (jnp.arange(edge, dtype=F32) - 9.0)[None, :, None]
    leaf_y = spread + (jnp.arange(edge, dtype=F32) - 9.0)[:, None, None]
    a0, a1, a2 = (places[:, :, n].astype(F32) for n in range(3))
    square = (a0 + leaf_x) ** 2 + (a1 + leaf_y) ** 2 + a2 * a2
    one = jnp.ones_like(spread)

    def in_three(value):
        high = lax.reduce_precision(value, 8, 7)
        middle = lax.reduce_precision(value - high, 8, 7)
        return [high, middle, value - high - middle]

    nothing = jnp.zeros_like(spread)
    target = [a0, a0, leaf_x, leaf_x, a1, a1, leaf_y, leaf_y, a2]
    target += in_three(square) + [one, one, one, nothing]
    source = [a0, leaf_x, a0, leaf_x, a1, leaf_y, a1, leaf_y, a2]
    source = [-2.0 * s for s in source] + [one, one, one]
    source += in_three(square + DELTA_SQ) + [nothing]

    def stack(parts):
        rows = jnp.stack([p.astype(BF16) for p in parts], axis=1)
        return rows.reshape(edge, 16, edge * 128)

    strength = [charges[:, :, n] for n in range(3)]
    return stack(target), stack(source), stack(strength * 2 + [nothing] * 10)


def body(weights, fold, unfold, steps, multipole, positions, strengths, vlist, ulist):
    del vlist
    eq_count, per_leaf = multipole.shape[1], positions.shape[1]
    occupied = ulist[4] >= 0
    held = occupied.astype(BF16)
    rows = jnp.concatenate(
        [
            (multipole * held).reshape(3 * eq_count, -1),
            positions.reshape(3 * per_leaf, -1),
            (strengths * held).reshape(3 * per_leaf, -1),
        ],
        axis=0,
    )
    square = rows.T.reshape(SIDE, SIDE, -1)
    wide = with_halo(square)
    eq = 3 * eq_count
    folded = jnp.einsum(
        "yxcj,jk->yxck",
        wide[..., :eq].reshape(WIDE, WIDE, 3, eq_count),
        fold,
        preferred_element_type=F32,
    ).astype(BF16)
    folded = jnp.pad(folded, ((0, 0), (0, 0), (0, 1), (0, 0)))
    by_parity = folded.reshape(WIDE // 2, 2, WIDE, 4, 2 * HALF).transpose(1, 0, 2, 3, 4)
    windows = jnp.stack([by_parity[:, :, x : x + SIDE - 1 : 2] for x in range(6)])
    windows = windows.reshape(12, WIDE // 2, 32, 2 * HALF)
    result = far_field(windows, weights, steps)
    result = result.reshape(2, 2, 8, 8, 4, 4 * HALF)[:, :, :, :, :3]
    result = result.transpose(4, 2, 0, 3, 1, 5).reshape(3, SIDE * SIDE, 4 * HALF)
    check = jnp.einsum("clk,ik->cil", result, unfold, preferred_element_type=F32)
    check = check * occupied.astype(F32)
    particles = wide[1:-1, 1:-1, eq:].reshape(SIDE + 2, SIDE + 2, 6, per_leaf)
    target, source, charge = near_inputs(particles[:, :, :3], particles[:, :, 3:])
    potential = near_field(target, source, charge)[:, :3]
    potential = potential.reshape(SIDE, 3, SIDE, per_leaf).transpose(1, 3, 0, 2)
    potential = potential.reshape(3, per_leaf, SIDE * SIDE) * occupied.astype(F32)
    return (check, potential)


def solution(mesh):
    leaves = P(None, None, ("morton", "slab"))
    lists = P(None, ("morton", "slab"))
    whole = [P(), P(), P(), P()]
    tables = far_tables()
    mapped = jax.shard_map(
        body,
        mesh=mesh,
        in_specs=(*whole, leaves, leaves, leaves, lists, lists),
        out_specs=(leaves, leaves),
        check_vma=False,
    )

    def run(multipole, positions, strengths, vlist, ulist):
        return mapped(*(jnp.asarray(t) for t in tables), multipole, positions, strengths, vlist, ulist)

    return run
```

time: 791 us -> 196 us (0.25); the launches traced: 779 us -> 194 us
  other arithmetic: 297 us -> 10.9 us
  local copies, waits for them, and re-layouts: 245 us -> 57.8 us
  loops' own time: 107 us -> 0 us
  Pallas kernels: 0 us -> 104 us
  matrix products: 101 us -> 5.71 us
  between operations: 17.1 us -> 0.89 us
    slice x156 -> x2, local copies, waits for them, and re-layouts: 188 us -> 0.18 us  [the longest x1 0.1 us: body(): wide[..., :eq].reshape(WIDE, WIDE, 3, eq_count)]
    reduce_sum x144 -> x0, other arithmetic: 128 us -> none  [row_potential(): summed = summed + jnp.sum(kernel_row[None] * charge[:, :, None, :], axis=-1)]
    div x48 -> x0, other arithmetic: 114 us -> none  [row_potential(): present[:, None, None] / (FOUR_PI * jnp.sqrt(squared + DELTA_SQ))]
    another operation x1 -> x0, loops' own time: 107 us -> none  [near_field(): lax.map(partial(row_potential, place, weight, lists, SIDE), jnp.arange(SI...]
    pallas_call x0 -> x2, Pallas kernels: none -> 104 us  [the longest x1 82.5 us: near_field(): pl.pallas_call(near_kernel, grid=(SIDE,), out_shape=jax.ShapeDtypeStruct(...]
    dot_general x108 -> x2, matrix products: 101 us -> 5.71 us  [the longest x1 3.31 us: body(): jnp.einsum('clk,ik->cil', result, unfold, preferred_element_type=F32)]
    another operation x0 -> x16, local copies, waits for them, and re-layouts: none -> 26.1 us  [the longest x15 25 us: stack(): rows = jnp.stack([p.astype(BF16) for p in parts], axis=1)]
    convert_element_type x135 -> x6, other arithmetic: 25 us -> 4.69 us  [the longest x4 3.28 us: stack(): rows = jnp.stack([p.astype(BF16) for p in parts], axis=1)]
  transfers between devices with their start and end apart: 6 -> 3, of which waited for: 1 -> 3; matrix products, arithmetic and copies ran while one was open for 42% -> 1% of each run, Pallas kernels for 0% -> 0%
where the time goes in v1:
time: 196 us; the launch traced here: 194 us
  Pallas kernels  104 us (53%)
  local copies, waits for them, and re-layouts  57.8 us (29%)
  other arithmetic  10.9 us (6%)
  starting transfers between devices  7.83 us (4%)
  waiting for transfers between devices  7.63 us (4%)
  matrix products  5.71 us (3%)
    pallas_call x1, Pallas kernels, near_field(): pl.pallas_call(near_kernel, grid=(SIDE,), out_shape=jax.ShapeDtypeStruct(...  82.5 us
    another operation x15, local copies, waits for them, and re-layouts, stack(): rows = jnp.stack([p.astype(BF16) for p in parts], axis=1)  25 us
    pallas_call x1, Pallas kernels, far_field(): pl.pallas_call(far_kernel, out_shape=jax.ShapeDtypeStruct((4, 256, 4 * HA...  21.2 us
    unnamed x16, local copies, waits for them, and re-layouts  10.1 us
    reshape x1, local copies, waits for them, and re-layouts, body(): windows = windows.reshape(12, WIDE // 2, 32, 2 * HALF)  7.2 us
    ppermute x1, waiting for transfers between devices, with_halo(): east = lax.ppermute(tall[:, :2], axes, westward)  5.29 us
    ppermute x1, starting transfers between devices, with_halo(): west = lax.ppermute(tall[:, -2:], axes, eastward)  4.61 us
    transpose x2, local copies, waits for them, and re-layouts, body(): result.transpose(4, 2, 0, 3, 1, 5).reshape(3, SIDE * SIDE, 4 * HALF)  4.33 us
  transfers between devices with their start and end apart: 3, of which 3 were waited for; matrix products, arithmetic and copies ran while one was open for 1% of the time, Pallas kernels for 0%

profile of v1, /device:TPU:3, one launch (start us, length us, event | category | flops | bytes accessed | tf_op | source)
XLA Modules:
  0.0 194.5 jit_solution(16150524602074629989)
XLA Ops:
  2.3 1.2 broadcast_multiply_fusion
  3.5 1.0 maximum_bitcast_fusion
  5.0 1.3 collective-permute-start
  7.9 1.9 collective-permute-done
  10.1 4.6 %collective-permute-start.1 = (bf16[20,2,2232]{2,1,0:T(2,128)(2,1)S(1)}, bf16[20,2,2232]{2,1,0:T(2,128)(2,1)S(1)}, u32[]{:S(2)}, u32[]{:S(2)}) collective-permute-start(bf16[20,2,2232]{2,1,0:T(2,128)(2,1)S(1)} %get-tuple-element.8), channel_id=1, source_target_pairs={{0,1},{2,3},{1,4},{3,6},{4,5},{6,7},{5,8},{7,10},{8,9},{10,11},{9,... | collective-permute-start | bytes 535688 | tf_op jit(solution)/shard_map/ppermute | solution.py:206
  14.7 1.9 collective-permute-start.2
  17.2 5.3 %collective-permute-done.2 = bf16[20,2,2232]{2,1,0:T(2,128)(2,1)S(1)} collective-permute-done((bf16[20,2,2232]{2,1,0:T(2,128)(2,1)S(1)}, bf16[20,2,2232]{2,1,0:T(2,128)(2,1)S(1)}, u32[]{:S(2)}, u32[]{:S(2)}) %collective-permute-start.2) | collective-permute-done | bytes 178592 | tf_op jit(solution)/shard_map/ppermute | solution.py:207
  23.9 1.5 pad_maximum_fusion
  25.6 2.9 %reshape.544 = bf16[20,20,3,488]{3,2,1,0:T(4,128)(2,1)} reshape(bf16[20,20,1464]{2,1,0:T(8,128)(2,1)S(1)} %slice.96) | data formatting | bytes 2342400 | tf_op jit(solution)/shard_map/reshape | solution.py:258
  28.5 2.4 %convolution_convert_fusion = bf16[20,20,3,512]{3,1,2,0:T(8,128)(2,1)S(1)} fusion(bf16[488,512,1,1]{1,0,3,2:T(8,128)(2,1)S(1)} %copy-done.4, bf16[20,20,3,488]{3,2,1,0:T(4,128)(2,1)} %reshape.544), kind=kOutput, calls=%fused_computation.2 | convolution fusion | flops 600268800 | bytes 2899712 | tf_op jit(solution)/shard_map/yxcj,jk->yxck/dot_general | solution.py:256
  31.2 2.0 %copy.61 = bf16[10,2,20,4,512]{4,3,2,0,1:T(4,128)(2,1)} copy(bf16[10,2,20,4,512]{4,2,3,1,0:T(8,128)(2,1)S(1)} %bitcast.89) | data formatting | bytes 3276800 | tf_op jit(solution)/shard_map/reshape | solution.py:263
  33.2 1.5 slice_bitcast_fusion.1
  34.7 1.8 multiply_convert_fusion
  36.5 1.5 reduce-precision_convert_fusion
  38.1 4.4 %stack.138.charge_ref = bf16[18,16,2304]{2,1,0:T(8,128)(2,1)S(1)} concatenate(bf16[18,1,2304]{2,1,0:T(2,128)(2,1)S(1)} %get-tuple-element.12, bf16[18,1,2304]{2,1,0:T(2,128)(2,1)S(1)} %get-tuple-element.11, bf16[18,1,2304]{2,1,0:T(2,128)(2,1)S(1)} %get-tuple-element.10, bf16[18,1,2304]{2,1,0:T(2,128)(2,1)S(1)} %get-tuple-element.12, bf16[18,1,2304]{2,1,0:T(2,128)(2,1)S(1)} %get-tuple-element.11, ...), dimensions={1} | concatenate | bytes 2654208 | tf_op jit(solution)/shard_map/stack | solution.py:233
  44.4 7.4 %stack.132.source_ref = bf16[18,16,2304]{2,1,0:T(8,128)(2,1)S(1)} concatenate(bf16[18,1,2304]{2,1,0:T(2,128)(2,1)S(1)} %get-tuple-element.20, bf16[18,1,2304]{2,1,0:T(2,128)(2,1)} %stack.130, bf16[18,1,2304]{2,1,0:T(2,128)(2,1)S(1)} %get-tuple-element.20, bf16[18,1,2304]{2,1,0:T(2,128)(2,1)} %stack.130, bf16[18,1,2304]{2,1,0:T(2,128)(2,1)S(1)} %get-tuple-element.17, ...), dimensions={1} | concatenate | bytes 2654208 | tf_op jit(solution)/shard_map/stack | solution.py:233
  52.0 9.3 %stack.127.target_ref = bf16[18,16,2304]{2,1,0:T(8,128)(2,1)} concatenate(bf16[18,1,2304]{2,1,0:T(2,128)(2,1)} %get-tuple-element.15, bf16[18,1,2304]{2,1,0:T(2,128)(2,1)} %get-tuple-element.15, bf16[18,1,2304]{2,1,0:T(2,128)(2,1)S(1)} %stack.120, bf16[18,1,2304]{2,1,0:T(2,128)(2,1)S(1)} %stack.120, bf16[18,1,2304]{2,1,0:T(2,128)(2,1)} %get-tuple-element.14, ...), dimensions={1} | concatenate | bytes 2654208 | tf_op jit(solution)/shard_map/stack | solution.py:233
  61.3 1.3 copy-done.1
  62.7 82.5 %near.1 = f32[16,8,2048]{2,1,0:T(8,128)S(1)} custom-call(bf16[18,16,2304]{2,1,0:T(8,128)(2,1)S(1)} %copy-done.1, bf16[18,16,2304]{2,1,0:T(8,128)(2,1)S(1)} %stack.132.source_ref, bf16[18,16,2304]{2,1,0:T(8,128)(2,1)S(1)} %stack.138.charge_ref), custom_call_target="tpu_custom_call" | custom-call | tf_op jit(solution)/shard_map/near/pallas_call | solution.py:179
  146.6 1.1 bitcast_dynamic-update-slice_fusion.5
  147.8 1.2 bitcast_dynamic-update-slice_fusion.4
  148.9 1.2 bitcast_dynamic-update-slice_fusion.3
  150.1 1.1 bitcast_dynamic-update-slice_fusion.2
  151.2 1.1 bitcast_dynamic-update-slice_fusion.1
  152.3 1.1 bitcast_dynamic-update-slice_fusion
  153.5 7.2 %reshape.546.windows = bf16[12,10,32,512]{3,2,1,0:T(8,128)(2,1)} reshape(bf16[6,2,10,8,4,512]{5,4,3,2,1,0:T(4,128)(2,1)} %bitcast_dynamic-update-slice_fusion) | data formatting | bytes 7864320 | tf_op jit(solution)/shard_map/reshape | solution.py:265
  160.7 2.1 %copy-done = bf16[12,10,32,512]{3,2,1,0:T(8,128)(2,1)S(1)} copy-done((bf16[12,10,32,512]{3,2,1,0:T(8,128)(2,1)S(1)}, bf16[12,10,32,512]{3,2,1,0:T(8,128)(2,1)}, u32[]{:S(2)}) %copy-start) | copy-done | bytes 3932184
  162.8 21.2 %far.1 = bf16[4,256,1024]{2,1,0:T(8,128)(2,1)S(1)} custom-call(s32[108,4]{1,0:T(8,128)S(1)} %copy-done.2, bf16[12,10,32,512]{3,2,1,0:T(8,128)(2,1)S(1)} %copy-done, bf16[40,2,256,256]{3,2,1,0:T(8,128)(2,1)} %constant.44.clone.weights), custom_call_target="tpu_custom_call" | custom-call | tf_op jit(solution)/shard_map/far/pallas_call | solution.py:117
  184.0 2.2 %reshape.547 = bf16[2,2,8,8,4,1024]{5,4,3,2,1,0:T(4,128)(2,1)} reshape(bf16[4,256,1024]{2,1,0:T(8,128)(2,1)S(1)} %far.1) | data formatting | bytes 4194304 | tf_op jit(solution)/shard_map/reshape | solution.py:267
  186.2 2.4 %slice_bitcast_fusion = bf16[3,8,2,8,2,1024]{5,0,3,1,4,2:T(4,128)(2,1)S(1)} fusion(bf16[2,2,8,8,4,1024]{5,4,3,2,1,0:T(4,128)(2,1)} %reshape.547), kind=kLoop, calls=%fused_computation.1 | loop fusion | bytes 3145728 | tf_op jit(solution)/shard_map/transpose | solution.py:268
  188.6 1.9 copy.39
  191.2 3.3 %multiply_bitcast_fusion = f32[3,488,256]{2,1,0:T(8,128)} fusion(bf16[3,256,1024]{2,1,0:T(8,128)(2,1)S(1)} %reshape.548, bf16[488,1024,1]{1,0,2:T(8,128)(2,1)} %constant.51, f32[256]{0:T(256)S(1)} %bitcast.95), kind=kOutput, calls=%fused_computation.4 | convolution fusion | flops 767932416 | bytes 4072448 | tf_op jit(solution)/shard_map/clk,ik->cil/dot_general | solution.py:269
  (42 shorter events, 10.7 us)
Async XLA Ops:
  5.0 4.8 %collective-permute-start = (bf16[2,16,2232]{2,1,0:T(8,128)(2,1)S(1)}, bf16[2,16,2232]{2,1,0:T(8,128)(2,1)S(1)}, u32[]{:S(2)}, u32[]{:S(2)}) collective-permute-start(bf16[2,16,2232]{2,1,0:T(8,128)(2,1)S(1)} %bitcast.93), channel_id=1, source_target_pairs={{0,2},{1,3},{2,0},{3,1},{4,6},{5,7},{6,4},{7,5},{8,10},{9,11},{10,... | collective-permute-start | bytes 428552 | tf_op jit(solution)/shard_map/ppermute | solution.py:194
  10.1 7.1 %collective-permute-start.1 = (bf16[20,2,2232]{2,1,0:T(2,128)(2,1)S(1)}, bf16[20,2,2232]{2,1,0:T(2,128)(2,1)S(1)}, u32[]{:S(2)}, u32[]{:S(2)}) collective-permute-start(bf16[20,2,2232]{2,1,0:T(2,128)(2,1)S(1)} %get-tuple-element.8), channel_id=1, source_target_pairs={{0,1},{2,3},{1,4},{3,6},{4,5},{6,7},{5,8},{7,10},{8,9},{10,11},{9,... | collective-permute-start | bytes 535688 | tf_op jit(solution)/shard_map/ppermute | solution.py:206
  14.7 7.8 %collective-permute-start.2 = (bf16[20,2,2232]{2,1,0:T(2,128)(2,1)S(1)}, bf16[20,2,2232]{2,1,0:T(2,128)(2,1)S(1)}, u32[]{:S(2)}, u32[]{:S(2)}) collective-permute-start(bf16[20,2,2232]{2,1,0:T(2,128)(2,1)S(1)} %get-tuple-element.9), channel_id=1, source_target_pairs={{1,0},{3,2},{4,1},{6,3},{5,4},{7,6},{8,5},{10,7},{9,8},{11,10},{12... | collective-permute-start | bytes 535688 | tf_op jit(solution)/shard_map/ppermute | solution.py:207
  25.6 2.9 %copy-start.4 = (bf16[488,512,1,1]{1,0,3,2:T(8,128)(2,1)S(1)}, bf16[488,512,1,1]{1,0,3,2:T(8,128)(2,1)}, u32[]{:S(2)}) copy-start(bf16[488,512,1,1]{1,0,3,2:T(8,128)(2,1)} %constant.50) | copy-start | bytes 1499140
  61.3 1.3 copy-start.1
  145.2 1.4 copy-start.3
  153.5 7.2 %copy-start.2 = (s32[108,4]{1,0:T(8,128)S(1)}, s32[108,4]{1,0:T(8,128)}, u32[]{:S(2)}) copy-start(s32[108,4]{1,0:T(8,128)} %constant.47.clone.steps) | copy-start | bytes 5188
  160.7 2.1 %copy-start = (bf16[12,10,32,512]{3,2,1,0:T(8,128)(2,1)S(1)}, bf16[12,10,32,512]{3,2,1,0:T(8,128)(2,1)}, u32[]{:S(2)}) copy-start(bf16[12,10,32,512]{3,2,1,0:T(8,128)(2,1)} %reshape.546.windows) | copy-start | bytes 11796484

commit v2 on v1

v2 whole, which is shorter than its diff:
```python
import math

import jax
import jax.numpy as jnp
import ml_dtypes
import numpy as np
from jax import lax
from jax.experimental import pallas as pl
from jax.experimental.pallas import tpu as pltpu
from jax.sharding import PartitionSpec as P

SIDE = 16
EQ_SIDE = 10
FOUR_PI = 4.0 * math.pi
DELTA_SQ = 0.01
RADIUS = 0.525
HALF = 256
WIDE = SIDE + 4
BF16 = jnp.bfloat16
F32 = jnp.float32


def surface_points():
    grid_line = np.linspace(-1.0, 1.0, EQ_SIDE)
    first, second, third = np.meshgrid(grid_line, grid_line, grid_line, indexing="ij")
    stacked = np.stack([first.ravel(), second.ravel(), third.ravel()], axis=1)
    on_face = np.max(np.abs(stacked), axis=1) > 0.999
    return (stacked[on_face] * RADIUS).astype(np.float32)


def translation(points, shift_x, shift_y):
    delta = points[:, None, :] - points[None, :, :]
    ex = delta[..., 0] - np.float32(shift_x)
    ey = delta[..., 1] - np.float32(shift_y)
    ez = delta[..., 2]
    distance = np.sqrt(ex * ex + ey * ey + ez * ez)
    table = (np.float32(1.0) / (np.float32(FOUR_PI) * distance)).astype(ml_dtypes.bfloat16)
    return table.astype(np.float32)


def mirror_halves(points):
    upper = np.nonzero(points[:, 2] > 0)[0]
    mirrored = points[upper] * np.array([1.0, 1.0, -1.0], np.float32)
    gap = np.abs(mirrored[:, None, :] - points[None, :, :]).max(-1)
    lower = gap.argmin(1)
    return upper, lower


def class_offsets(parity_x, parity_y):
    listed = []
    for shift_x in range(-2 - parity_x, 4 - parity_x):
        for shift_y in range(-2 - parity_y, 4 - parity_y):
            if abs(shift_x) > 1 or abs(shift_y) > 1:
                listed.append((shift_x, shift_y))
    return listed


def far_tables():
    points = surface_points()
    upper, lower = mirror_halves(points)
    half, count = len(upper), len(points)
    offsets = [(x, y) for x in range(-3, 4) for y in range(-3, 4) if max(abs(x), abs(y)) > 1]
    weights = np.zeros((len(offsets), 2, HALF, HALF), ml_dtypes.bfloat16)
    for n, (x, y) in enumerate(offsets):
        table = translation(points, x, y)
        same = table[np.ix_(upper, upper)]
        cross = table[np.ix_(upper, lower)]
        weights[n, 0, :half, :half] = (same + cross).T
        weights[n, 1, :half, :half] = (same - cross).T
    fold = np.zeros((count, 2 * HALF), np.float32)
    cols = np.arange(half)
    fold[upper, cols] = 1
    fold[lower, cols] = 1
    fold[upper, HALF + cols] = 1
    fold[lower, HALF + cols] = -1
    unfold = np.concatenate([fold, fold], axis=1) * 0.5
    steps = []
    for n, (x, y) in enumerate(offsets):
        for parity_y in (0, 1):
            for parity_x in (0, 1):
                if (x, y) in class_offsets(parity_x, parity_y):
                    start_x, start_y = 2 + parity_x + x, 2 + parity_y + y
                    steps.append(
                        (n, start_x * 6 + start_y, parity_y * 2 + parity_x)
                    )
    steps = np.array(sorted(steps, key=lambda step: step[2]), np.int32)
    return weights, fold.astype(ml_dtypes.bfloat16), unfold.astype(ml_dtypes.bfloat16), steps


def far_kernel(steps, wide, weights, unfold, occupied, out, rows, windows, sums):
    def widen(y, carry):
        for tile in range(12):
            rows[tile, y] = wide[y, :, tile * 128 : tile * 128 + 128].astype(F32)
        return carry

    lax.fori_loop(0, WIDE, widen, 0)

    def gather(start_y, carry):
        for start_x in range(6):
            for pair in range(4):
                for tile in range(12):
                    first = rows[tile, start_y + 4 * pair, pl.ds(start_x, 8, stride=2), :]
                    second = rows[tile, start_y + 4 * pair + 2, pl.ds(start_x, 8, stride=2), :]
                    at = tile // 4 * 64 + pair * 16
                    cols = slice(tile % 4 * 128, tile % 4 * 128 + 128)
                    windows[start_x * 6 + start_y, at : at + 16, cols] = jnp.concatenate(
                        [first, second], axis=0
                    ).astype(BF16)
        return carry

    lax.fori_loop(0, 6, gather, 0)

    def one_class(n, carry):
        for e in range(2):
            cols = slice(e * HALF, (e + 1) * HALF)
            sources = [windows[steps[n * 27 + k, 1], :, cols] for k in range(27)]
            tables = [weights[steps[n * 27 + k, 0], e] for k in range(27)]
            value = jnp.dot(
                jnp.concatenate(sources, axis=1),
                jnp.concatenate(tables, axis=0),
                preferred_element_type=F32,
            )
            for c in range(3):
                for a in range(8):
                    at = c * 64 + a * 8
                    for b in range(2):
                        sums[
                            e * 2 + b, c * SIDE + 2 * a + n // 2, pl.ds(n % 2, 8, stride=2), :
                        ] = value[at : at + 8, b * 128 : b * 128 + 128]
        return carry

    lax.fori_loop(0, 4, one_class, 0)
    for c in range(3):
        value = jnp.concatenate(
            [sums[n, c * SIDE : (c + 1) * SIDE].reshape(SIDE * SIDE, 128) for n in range(4)],
            axis=1,
        )
        high = value.astype(BF16)
        low = (value - high.astype(F32)).astype(BF16)
        out[c] = (
            lax.dot_general(
                unfold[...],
                jnp.concatenate([high, low], axis=1),
                (((1,), (1,)), ((), ())),
                preferred_element_type=F32,
            )
            * occupied[...]
        )


def far_field(wide, weights, unfold, steps, occupied):
    count = unfold.shape[0]
    vmem = pl.BlockSpec(memory_space=pltpu.VMEM)
    return pl.pallas_call(
        far_kernel,
        out_shape=jax.ShapeDtypeStruct((3, count, SIDE * SIDE), F32),
        in_specs=[pl.BlockSpec(memory_space=pltpu.SMEM), vmem, vmem, vmem, vmem],
        out_specs=vmem,
        scratch_shapes=[
            pltpu.VMEM((12, WIDE, WIDE, 128), F32),
            pltpu.VMEM((36, 192, 2 * HALF), BF16),
            pltpu.VMEM((4, 3 * SIDE, SIDE, 128), F32),
        ],
        compiler_params=pltpu.CompilerParams(vmem_limit_bytes=50 * 2**20),
        name="far",
    )(steps, wide, weights, unfold, occupied)


def near_selection():
    target = [(0, 1), (0, 1), (6, 1), (6, 1), (1, 1), (1, 1), (7, 1), (7, 1), (2, 1)]
    target += [(8, 1), (9, 1), (10, 1), (14, 1), (14, 1), (14, 1), (15, 1)]
    source = [(0, -2), (6, -2), (0, -2), (6, -2), (1, -2), (7, -2), (1, -2), (7, -2), (2, -2)]
    source += [(14, 1), (14, 1), (14, 1), (11, 1), (12, 1), (13, 1), (15, 1)]
    charge = [(3, 1), (4, 1), (5, 1)] * 2 + [(15, 1)] * 10
    table = np.zeros((48, 16), np.float32)
    for row, (column, value) in enumerate(target + source + charge):
        table[row, column] = value
    return table.astype(ml_dtypes.bfloat16)


def near_kernel(select_ref, particle_ref, out_ref, factor_ref):
    y = pl.program_id(0)
    leaf = 128
    first_three = lax.broadcasted_iota(jnp.int32, (16, leaf), 0) < 3
    left_half = lax.broadcasted_iota(jnp.int32, (16, 2 * leaf), 1) < leaf
    contract = (((0,), (0,)), ((), ()))
    lanes = particle_ref.shape[-1]

    @pl.when(y == 0)
    def _():
        line = lax.broadcasted_iota(jnp.int32, (8, lanes), 0)
        column = lax.broadcasted_iota(jnp.int32, (8, lanes), 1) // leaf
        leaf_x = column.astype(F32) - 9.0

        def in_three(value):
            high = value.astype(BF16).astype(F32)
            middle = (value - high).astype(BF16).astype(F32)
            return [high, middle, value - high - middle]

        def factors(row, carry):
            leaf_y = row.astype(F32) - 9.0
            held = particle_ref[row].astype(F32)
            upper = jnp.where(line == 6, leaf_x, jnp.where(line == 7, leaf_y, held))
            place_x = held[0:1] + leaf_x[0:1]
            place_y = held[1:2] + leaf_y
            square = place_x * place_x + place_y * place_y + held[2:3] * held[2:3]
            parts = in_three(square) + in_three(square + DELTA_SQ)
            lower = jnp.where(line == 6, 1.0, 0.0)
            for n, part in enumerate(parts):
                lower = jnp.where(line == n, part, lower)
            base = jnp.concatenate([upper, lower], axis=0).astype(BF16)
            factor_ref[row] = jnp.dot(
                select_ref[...], base, preferred_element_type=F32
            ).astype(BF16)
            return carry

        lax.fori_loop(0, SIDE + 2, factors, 0)

    def pair(i, carry):
        base = pl.multiple_of(i * 2 * leaf, 2 * leaf)
        target = factor_ref[y + 1, 0:16, pl.ds(base + leaf, 2 * leaf)]
        nothing = jnp.zeros((16, leaf), BF16)
        split = jnp.concatenate(
            [
                jnp.concatenate([target[:, :leaf], nothing], axis=1),
                jnp.concatenate([nothing, target[:, leaf:]], axis=1),
            ],
            axis=0,
        )
        inverses, charges = [], []
        for k in range(3):
            source = factor_ref[y + k, 16:32, pl.ds(base, 4 * leaf)]
            charge = factor_ref[y + k, 32:48, pl.ds(base, 4 * leaf)]
            middle = lax.dot_general(
                source[:, leaf : 3 * leaf], target, contract, preferred_element_type=F32
            )
            outer = jnp.concatenate([source[:, :leaf], source[:, 3 * leaf :]], axis=0)
            edge = lax.dot_general(outer, split, contract, preferred_element_type=F32)
            inverses += [lax.rsqrt(middle.astype(BF16)), lax.rsqrt(edge.astype(BF16))]
            charges += [
                charge[:, leaf : 3 * leaf],
                jnp.where(first_three, charge[:, :leaf], charge[:, 3 * leaf :]),
            ]
        total = jnp.dot(
            jnp.concatenate(charges, axis=1),
            jnp.concatenate(inverses, axis=0),
            preferred_element_type=F32,
        )
        chosen = jnp.where(left_half, total, pltpu.roll(total, 16 - 3, 0))
        out_ref[0, :, pl.ds(base, 2 * leaf)] = chosen[:8] * (1.0 / FOUR_PI)
        return carry

    lax.fori_loop(0, SIDE // 2, pair, 0, unroll=4)


def near_field(select, particles):
    lanes = particles.shape[-1]
    return pl.pallas_call(
        near_kernel,
        grid=(SIDE,),
        out_shape=jax.ShapeDtypeStruct((SIDE, 8, SIDE * 128), F32),
        in_specs=[
            pl.BlockSpec((48, 16), lambda y: (0, 0)),
            pl.BlockSpec((SIDE + 2, 8, lanes), lambda y: (0, 0, 0)),
        ],
        out_specs=pl.BlockSpec((1, 8, SIDE * 128), lambda y: (y, 0, 0)),
        scratch_shapes=[pltpu.VMEM((SIDE + 2, 48, lanes), BF16)],
        compiler_params=pltpu.CompilerParams(vmem_limit_bytes=40 * 2**20),
        name="near",
    )(select, particles)


def with_halo(square):
    tiles = lax.axis_size("morton")
    quad_y = lax.axis_index("slab") // 2
    sent = jnp.where(quad_y == 0, square[-2:], square[:2])
    other = lax.ppermute(sent, "slab", [(0, 2), (1, 3), (2, 0), (3, 1)])
    blank = jnp.zeros_like(other)
    below = jnp.where(quad_y == 0, blank, other)
    above = jnp.where(quad_y == 0, other, blank)
    tall = jnp.concatenate([below, square, above], axis=0)

    def index(x, y):
        return (x // 2) * 4 + 2 * y + x % 2

    eastward = [(index(x, y), index(x + 1, y)) for x in range(2 * tiles - 1) for y in (0, 1)]
    westward = [(b, a) for a, b in eastward]
    axes = ("morton", "slab")
    west = lax.ppermute(tall[:, -2:], axes, eastward)
    east = lax.ppermute(tall[:, :2], axes, westward)
    return jnp.concatenate([west, tall, east], axis=1)


def body(weights, fold, unfold, steps, select, multipole, positions, strengths, vlist, ulist):
    del vlist
    per_leaf = positions.shape[1]
    occupied = ulist[4] >= 0
    held = occupied.astype(BF16)
    folded = jnp.einsum(
        "cjl,jk->clk", multipole * held, fold, preferred_element_type=F32
    ).astype(BF16)
    particles = jnp.concatenate([positions, strengths * held], axis=0)
    particles = particles.reshape(6 * per_leaf, -1).T
    square = jnp.concatenate([folded[0], folded[1], folded[2], particles], axis=1)
    wide = with_halo(square.reshape(SIDE, SIDE, -1))
    eq = 6 * HALF
    kept = occupied.astype(F32)
    check = far_field(wide[..., :eq], weights, unfold, steps, kept[None])
    particles = wide[1:-1, 1:-1, eq:].reshape(SIDE + 2, SIDE + 2, 6, per_leaf)
    particles = jnp.pad(particles.transpose(0, 2, 1, 3), ((0, 0), (0, 2), (0, 0), (0, 0)))
    potential = near_field(select, particles.reshape(SIDE + 2, 8, -1))[:, :3]
    potential = potential.reshape(SIDE, 3, SIDE, per_leaf).transpose(1, 3, 0, 2)
    potential = potential.reshape(3, per_leaf, SIDE * SIDE) * kept
    return (check, potential)


def solution(mesh):
    leaves = P(None, None, ("morton", "slab"))
    lists = P(None, ("morton", "slab"))
    whole = [P()] * 5
    tables = (*far_tables(), near_selection())
    mapped = jax.shard_map(
        body,
        mesh=mesh,
        in_specs=(*whole, leaves, leaves, leaves, lists, lists),
        out_specs=(leaves, leaves),
        check_vma=False,
    )

    def run(multipole, positions, strengths, vlist, ulist):
        return mapped(*(jnp.asarray(t) for t in tables), multipole, positions, strengths, vlist, ulist)

    return run
```

time: 196 us -> 90.8 us (0.46)
  local copies, waits for them, and re-layouts: 57.8 us -> 6.27 us
  Pallas kernels: 104 us -> 60.5 us
  other arithmetic: 10.9 us -> 4.53 us
  matrix products: 5.71 us -> 1.91 us
    pallas_call x1, Pallas kernels: 82.5 us -> 46.7 us  [near_field(): pl.pallas_call(near_kernel, grid=(SIDE,), out_shape=jax.ShapeDtypeStruct(...]
    another operation x16 -> x0, local copies, waits for them, and re-layouts: 26.1 us -> none  [the longest x15 25 us: stack(): rows = jnp.stack([p.astype(BF16) for p in parts], axis=1)]
    reshape x5 -> x2, local copies, waits for them, and re-layouts: 15 us -> 1.37 us  [the longest x1 1.2 us: body(): potential = near_field(select, particles.reshape(SIDE + 2, 8, -1))[:, :3]]
    unnamed x16 -> x11, local copies, waits for them, and re-layouts: 10.1 us -> 0.94 us
    pallas_call x1, Pallas kernels: 21.2 us -> 13.8 us  [far_field(): pl.pallas_call(far_kernel, out_shape=jax.ShapeDtypeStruct((3, count, SIDE...]
    transpose x3 -> x0, local copies, waits for them, and re-layouts: 5.05 us -> none  [the longest x2 4.33 us: body(): result.transpose(4, 2, 0, 3, 1, 5).reshape(3, SIDE * SIDE, 4 * HALF)]
    dot_general x2 -> x1, matrix products: 5.71 us -> 1.91 us  [body(): jnp.einsum('cjl,jk->clk', multipole * held, fold, preferred_element_type=...]
    convert_element_type x5 -> x1, other arithmetic: 3.98 us -> 0.7 us  [body(): kept = occupied.astype(F32)]
  transfers between devices with their start and end apart: 3 -> 3, of which waited for: 3 -> 2; matrix products, arithmetic and copies ran while one was open for 1% -> 1% of each run, Pallas kernels for 0% -> 0%
where the time goes in v2:
time: 90.8 us; the launch traced here: 90.4 us
  Pallas kernels  60.5 us (67%)
  waiting for transfers between devices  8.61 us (9%)
  starting transfers between devices  7.81 us (9%)
  local copies, waits for them, and re-layouts  6.27 us (7%)
  other arithmetic  4.53 us (5%)
  matrix products  1.91 us (2%)
    pallas_call x1, Pallas kernels, near_field(): pl.pallas_call(near_kernel, grid=(SIDE,), out_shape=jax.ShapeDtypeStruct(...  46.7 us
    pallas_call x1, Pallas kernels, far_field(): pl.pallas_call(far_kernel, out_shape=jax.ShapeDtypeStruct((3, count, SIDE...  13.8 us
    ppermute x1, waiting for transfers between devices, with_halo(): east = lax.ppermute(tall[:, :2], axes, westward)  5.12 us
    ppermute x1, starting transfers between devices, with_halo(): west = lax.ppermute(tall[:, -2:], axes, eastward)  4.59 us
    ppermute x1, waiting for transfers between devices, with_halo(): other = lax.ppermute(sent, 'slab', [(0, 2), (1, 3), (2, 0), (3, 1)])  3.49 us
    concatenate x1, other arithmetic, with_halo(): return jnp.concatenate([west, tall, east], axis=1)  2.55 us
    reshape x2, local copies, waits for them, and re-layouts, body(): potential = potential.reshape(SIDE, 3, SIDE, per_leaf).transpose(1, 3, 0, 2)  2.04 us
    ppermute x1, starting transfers between devices, with_halo(): east = lax.ppermute(tall[:, :2], axes, westward)  1.92 us
  transfers between devices with their start and end apart: 3, of which 2 were waited for; matrix products, arithmetic and copies ran while one was open for 1% of the time, Pallas kernels for 0%

profile of v2, /device:TPU:3, one launch (start us, length us, event | category | flops | bytes accessed | tf_op | source)
XLA Modules:
  0.0 90.4 jit_solution(10694793057020950734)
XLA Ops:
  0.6 0.0 copy-start.3
  0.6 0.0 copy-start.4
  0.7 0.8 fusion.3
  1.4 1.9 %convolution_convert_fusion = bf16[3,256,512]{2,1,0:T(8,128)(2,1)S(1)} fusion(bf16[488,512,1]{1,0,2:T(8,128)(2,1)} %constant.40, bf16[3,488,256]{2,1,0:T(8,128)(2,1)} %param.10, bf16[256]{0:T(256)(128)(2,1)S(1)} %fusion.3), kind=kOutput, calls=%fused_computation.1 | convolution fusion | flops 384546816 | bytes 2036224 | tf_op jit(solution)/shard_map/cjl,jk->clk/dot_general | solution.py:299
  3.3 0.1 fusion.4
  3.5 0.0 copy-done.3
  3.6 0.2 copy.13
  3.8 1.3 %collective-permute-start = (bf16[2,16,2304]{2,1,0:T(8,128)(2,1)S(1)}, bf16[2,16,2304]{2,1,0:T(8,128)(2,1)S(1)}, u32[]{:S(2)}, u32[]{:S(2)}) collective-permute-start(bf16[2,16,2304]{2,1,0:T(8,128)(2,1)S(1)} %bitcast.36), channel_id=1, source_target_pairs={{0,2},{1,3},{2,0},{3,1},{4,6},{5,7},{6,4},{7,5},{8,10},{9,11},{10,... | collective-permute-start | bytes 442376 | tf_op jit(solution)/shard_map/ppermute | solution.py:277
  5.1 3.5 %collective-permute-done = bf16[2,16,2304]{2,1,0:T(8,128)(2,1)S(1)} collective-permute-done((bf16[2,16,2304]{2,1,0:T(8,128)(2,1)S(1)}, bf16[2,16,2304]{2,1,0:T(8,128)(2,1)S(1)}, u32[]{:S(2)}, u32[]{:S(2)}) %collective-permute-start) | collective-permute-done | bytes 147488 | tf_op jit(solution)/shard_map/ppermute | solution.py:277
  8.6 0.3 pad_maximum_fusion.7
  8.9 4.6 %collective-permute-start.1 = (bf16[20,2,2304]{2,1,0:T(2,128)(2,1)S(1)}, bf16[20,2,2304]{2,1,0:T(2,128)(2,1)S(1)}, u32[]{:S(2)}, u32[]{:S(2)}) collective-permute-start(bf16[20,2,2304]{2,1,0:T(2,128)(2,1)S(1)} %get-tuple-element.4), channel_id=1, source_target_pairs={{0,1},{2,3},{1,4},{3,6},{4,5},{6,7},{5,8},{7,10},{8,9},{10,11},{9,... | collective-permute-start | bytes 552968 | tf_op jit(solution)/shard_map/ppermute | solution.py:289
  13.5 1.9 %collective-permute-start.2 = (bf16[20,2,2304]{2,1,0:T(2,128)(2,1)S(1)}, bf16[20,2,2304]{2,1,0:T(2,128)(2,1)S(1)}, u32[]{:S(2)}, u32[]{:S(2)}) collective-permute-start(bf16[20,2,2304]{2,1,0:T(2,128)(2,1)S(1)} %get-tuple-element.5), channel_id=1, source_target_pairs={{1,0},{3,2},{4,1},{6,3},{5,4},{7,6},{8,5},{10,7},{9,8},{11,10},{12... | collective-permute-start | bytes 552968 | tf_op jit(solution)/shard_map/ppermute | solution.py:290
  15.4 0.7 compare_convert_fusion.occupied
  16.2 0.0 collective-permute-done.1
  16.2 5.1 %collective-permute-done.2 = bf16[20,2,2304]{2,1,0:T(2,128)(2,1)S(1)} collective-permute-done((bf16[20,2,2304]{2,1,0:T(2,128)(2,1)S(1)}, bf16[20,2,2304]{2,1,0:T(2,128)(2,1)S(1)}, u32[]{:S(2)}, u32[]{:S(2)}) %collective-permute-start.2) | collective-permute-done | bytes 184352 | tf_op jit(solution)/shard_map/ppermute | solution.py:290
  21.3 2.5 %pad_maximum_fusion = bf16[20,20,2304]{2,1,0:T(8,128)(2,1)S(1)} fusion(bf16[20,2,2304]{2,1,0:T(2,128)(2,1)S(1)} %collective-permute-done.2, bf16[2,16,2304]{2,1,0:T(8,128)(2,1)S(1)} %get-tuple-element.13, bf16[16,16,768]{2,1,0:T(8,128)(2,1)S(1)} %bitcast.27, bf16[16,16,512]{2,1,0:T(8,128)(2,1)S(1)} %bitcast.32, bf16[16,16,512]{2,1,0:T(8,128)(2,1)S(1)} %bitcast.34, ...), kind=kLoop, calls=%fused_computation | loop fusion | flops 14745600 | bytes 3686400 | tf_op jit(solution)/shard_map/concatenate | solution.py:291
  23.8 0.0 copy-start.2
  23.8 0.2 slice.50
  24.0 0.1 slice.49.wide
  24.1 0.0 copy-start
  24.2 0.0 copy-start.1
  24.2 1.4 %reshape.48 = bf16[18,18,6,128]{3,2,1,0:T(8,128)(2,1)} reshape(bf16[18,18,768]{2,1,0:T(8,128)(2,1)S(1)} %slice.50) | data formatting | bytes 995328 | tf_op jit(solution)/shard_map/reshape | solution.py:309
  25.6 1.2 %pad_bitcast_fusion.particle_ref = bf16[18,8,2304]{2,1,0:T(8,128)(2,1)S(1)} fusion(bf16[18,6,18,128]{3,1,2,0:T(8,128)(2,1)} %bitcast.28), kind=kLoop, calls=%fused_computation.3 | loop fusion | bytes 1161216 | tf_op jit(solution)/shard_map/reshape | solution.py:311
  26.8 0.0 copy-done.2
  26.8 46.7 %near.1 = f32[16,8,2048]{2,1,0:T(8,128)S(1)} custom-call(bf16[48,16]{1,0:T(8,128)(2,1)S(1)} %copy-done.2, bf16[18,8,2304]{2,1,0:T(8,128)(2,1)S(1)} %pad_bitcast_fusion.particle_ref), custom_call_target="tpu_custom_call" | custom-call | tf_op jit(solution)/shard_map/near/pallas_call | solution.py:258
  73.5 0.1 slice.51
  73.6 1.0 %reshape.55 = f32[16,3,16,128]{3,2,1,0:T(8,128)} reshape(f32[16,3,2048]{2,1,0:T(4,128)S(1)} %slice.51) | data formatting | bytes 786432 | tf_op jit(solution)/shard_map/reshape | solution.py:312
  74.6 1.0 %copy.16 = f32[16,3,16,128]{3,2,0,1:T(8,128)S(1)} copy(f32[16,3,16,128]{3,2,1,0:T(8,128)} %reshape.55) | data formatting | bytes 786432 | tf_op jit(solution)/shard_map/reshape | solution.py:312
  75.6 0.1 bitcast_multiply_fusion
  75.7 0.9 %copy.15 = f32[3,128,256]{2,1,0:T(8,128)} copy(f32[3,128,256]{1,2,0:T(8,128)S(1)} %bitcast_multiply_fusion) | data formatting | bytes 786432
  76.6 0.0 copy-done.1
  76.6 13.8 %far.1 = f32[3,488,256]{2,1,0:T(8,128)} custom-call(s32[108,3]{1,0:T(8,128)S(1)} %copy-done.1, bf16[20,20,1536]{2,1,0:T(8,128)(2,1)S(1)} %slice.49.wide, bf16[40,2,256,256]{3,2,1,0:T(8,128)(2,1)} %constant.33.clone.weights, bf16[488,1024]{1,0:T(8,128)(2,1)S(1)} %copy-done, f32[1,256]{1,0:T(1,128)S(1)} %compare_convert_fusion.occupied), custom_call_target="tpu_custom_call" | custom-call | tf_op jit(solution)/shard_map/far/pallas_call | solution.py:154
  (6 shorter events, 0.1 us)
Async XLA Ops:
  0.6 2.9 %copy-start.3 = (bf16[3,128,256]{2,1,0:T(8,128)(2,1)S(1)}, bf16[3,128,256]{2,1,0:T(8,128)(2,1)}, u32[]{:S(2)}) copy-start(bf16[3,128,256]{2,1,0:T(8,128)(2,1)} %param.12) | copy-start | bytes 589828
  0.6 2.9 %copy-start.4 = (bf16[3,128,256]{2,1,0:T(8,128)(2,1)S(1)}, bf16[3,128,256]{2,1,0:T(8,128)(2,1)}, u32[]{:S(2)}) copy-start(bf16[3,128,256]{2,1,0:T(8,128)(2,1)} %param.11) | copy-start | bytes 589828
  3.8 4.8 %collective-permute-start = (bf16[2,16,2304]{2,1,0:T(8,128)(2,1)S(1)}, bf16[2,16,2304]{2,1,0:T(8,128)(2,1)S(1)}, u32[]{:S(2)}, u32[]{:S(2)}) collective-permute-start(bf16[2,16,2304]{2,1,0:T(8,128)(2,1)S(1)} %bitcast.36), channel_id=1, source_target_pairs={{0,2},{1,3},{2,0},{3,1},{4,6},{5,7},{6,4},{7,5},{8,10},{9,11},{10,... | collective-permute-start | bytes 442376 | tf_op jit(solution)/shard_map/ppermute | solution.py:277
  8.9 7.2 %collective-permute-start.1 = (bf16[20,2,2304]{2,1,0:T(2,128)(2,1)S(1)}, bf16[20,2,2304]{2,1,0:T(2,128)(2,1)S(1)}, u32[]{:S(2)}, u32[]{:S(2)}) collective-permute-start(bf16[20,2,2304]{2,1,0:T(2,128)(2,1)S(1)} %get-tuple-element.4), channel_id=1, source_target_pairs={{0,1},{2,3},{1,4},{3,6},{4,5},{6,7},{5,8},{7,10},{8,9},{10,11},{9,... | collective-permute-start | bytes 552968 | tf_op jit(solution)/shard_map/ppermute | solution.py:289
  13.5 7.8 %collective-permute-start.2 = (bf16[20,2,2304]{2,1,0:T(2,128)(2,1)S(1)}, bf16[20,2,2304]{2,1,0:T(2,128)(2,1)S(1)}, u32[]{:S(2)}, u32[]{:S(2)}) collective-permute-start(bf16[20,2,2304]{2,1,0:T(2,128)(2,1)S(1)} %get-tuple-element.5), channel_id=1, source_target_pairs={{1,0},{3,2},{4,1},{6,3},{5,4},{7,6},{8,5},{10,7},{9,8},{11,10},{12... | collective-permute-start | bytes 552968 | tf_op jit(solution)/shard_map/ppermute | solution.py:290
  23.8 3.0 %copy-start.2 = (bf16[48,16]{1,0:T(8,128)(2,1)S(1)}, bf16[48,16]{1,0:T(8,128)(2,1)}, u32[]{:S(2)}) copy-start(bf16[48,16]{1,0:T(8,128)(2,1)} %constant.37.clone.select_ref) | copy-start | bytes 4612
  24.1 52.5 %copy-start = (bf16[488,1024]{1,0:T(8,128)(2,1)S(1)}, bf16[488,1024]{1,0:T(8,128)(2,1)}, u32[]{:S(2)}) copy-start(bf16[488,1024]{1,0:T(8,128)(2,1)} %constant.35.clone.unfold) | copy-start | bytes 2998276
  24.2 52.5 %copy-start.1 = (s32[108,3]{1,0:T(8,128)S(1)}, s32[108,3]{1,0:T(8,128)}, u32[]{:S(2)}) copy-start(s32[108,3]{1,0:T(8,128)} %constant.36.clone.steps) | copy-start | bytes 3892

commit v3 on v2

--- a/solution.py
+++ b/solution.py
@@ -250,7 +250,7 @@
         out_ref[0, :, pl.ds(base, 2 * leaf)] = chosen[:8] * (1.0 / FOUR_PI)
         return carry
 
-    lax.fori_loop(0, SIDE // 2, pair, 0, unroll=4)
+    lax.fori_loop(0, SIDE // 2, pair, 0, unroll=8)
 
 
 def near_field(select, particles):
@@ -266,14 +266,17 @@
         out_specs=pl.BlockSpec((1, 8, SIDE * 128), lambda y: (y, 0, 0)),
         scratch_shapes=[pltpu.VMEM((SIDE + 2, 48, lanes), BF16)],
         compiler_params=pltpu.CompilerParams(vmem_limit_bytes=40 * 2**20),
+        cost_estimate=pl.CostEstimate(
+            flops=40_000_000_000, bytes_accessed=2_000_000, transcendentals=0
+        ),
         name="near",
     )(select, particles)
 
 
-def with_halo(square):
+def with_halo(square, halo):
     tiles = lax.axis_size("morton")
     quad_y = lax.axis_index("slab") // 2
-    sent = jnp.where(quad_y == 0, square[-2:], square[:2])
+    sent = jnp.where(quad_y == 0, square[-halo:], square[:halo])
     other = lax.ppermute(sent, "slab", [(0, 2), (1, 3), (2, 0), (3, 1)])
     blank = jnp.zeros_like(other)
     below = jnp.where(quad_y == 0, blank, other)
@@ -286,8 +289,8 @@
     eastward = [(index(x, y), index(x + 1, y)) for x in range(2 * tiles - 1) for y in (0, 1)]
     westward = [(b, a) for a, b in eastward]
     axes = ("morton", "slab")
-    west = lax.ppermute(tall[:, -2:], axes, eastward)
-    east = lax.ppermute(tall[:, :2], axes, westward)
+    west = lax.ppermute(tall[:, -halo:], axes, eastward)
+    east = lax.ppermute(tall[:, :halo], axes, westward)
     return jnp.concatenate([west, tall, east], axis=1)
 
 
@@ -296,19 +299,18 @@
     per_leaf = positions.shape[1]
     occupied = ulist[4] >= 0
     held = occupied.astype(BF16)
+    particles = jnp.concatenate([positions, strengths * held], axis=0)
+    particles = particles.reshape(6 * per_leaf, -1).T.reshape(SIDE, SIDE, -1)
+    particles = with_halo(particles, 1).reshape(SIDE + 2, SIDE + 2, 6, per_leaf)
+    particles = jnp.pad(particles.transpose(0, 2, 1, 3), ((0, 0), (0, 2), (0, 0), (0, 0)))
     folded = jnp.einsum(
         "cjl,jk->clk", multipole * held, fold, preferred_element_type=F32
     ).astype(BF16)
-    particles = jnp.concatenate([positions, strengths * held], axis=0)
-    particles = particles.reshape(6 * per_leaf, -1).T
-    square = jnp.concatenate([folded[0], folded[1], folded[2], particles], axis=1)
-    wide = with_halo(square.reshape(SIDE, SIDE, -1))
-    eq = 6 * HALF
+    square = jnp.concatenate([folded[0], folded[1], folded[2]], axis=1)
+    wide = with_halo(square.reshape(SIDE, SIDE, -1), 2)
     kept = occupied.astype(F32)
-    check = far_field(wide[..., :eq], weights, unfold, steps, kept[None])
-    particles = wide[1:-1, 1:-1, eq:].reshape(SIDE + 2, SIDE + 2, 6, per_leaf)
-    particles = jnp.pad(particles.transpose(0, 2, 1, 3), ((0, 0), (0, 2), (0, 0), (0, 0)))
     potential = near_field(select, particles.reshape(SIDE + 2, 8, -1))[:, :3]
+    check = far_field(wide, weights, unfold, steps, kept[None])
     potential = potential.reshape(SIDE, 3, SIDE, per_leaf).transpose(1, 3, 0, 2)
     potential = potential.reshape(3, per_leaf, SIDE * SIDE) * kept
     return (check, potential)

time: 90.8 us -> 87.3 us (0.961)
  the two profiles are of different devices: /device:TPU:3 before, /device:TPU:24 now
where the time goes in v3:
time: 87.3 us; the launch traced here: 86.9 us
  Pallas kernels  55.4 us (63%)
  waiting for transfers between devices  11.5 us (13%)
  starting transfers between devices  10.8 us (12%)
  other arithmetic  5.13 us (6%)
  local copies, waits for them, and re-layouts  2.54 us (3%)
    pallas_call x1, Pallas kernels, near_field(): pl.pallas_call(near_kernel, grid=(SIDE,), out_shape=jax.ShapeDtypeStruct(...  41.6 us
    pallas_call x1, Pallas kernels, far_field(): pl.pallas_call(far_kernel, out_shape=jax.ShapeDtypeStruct((3, count, SIDE...  13.8 us
    ppermute x2, waiting for transfers between devices, with_halo(): west = lax.ppermute(tall[:, -halo:], axes, eastward)  6.91 us
    ppermute x2, starting transfers between devices, with_halo(): west = lax.ppermute(tall[:, -halo:], axes, eastward)  4.81 us
    ppermute x2, waiting for transfers between devices, with_halo(): other = lax.ppermute(sent, 'slab', [(0, 2), (1, 3), (2, 0), (3, 1)])  4.58 us
    ppermute x2, starting transfers between devices, with_halo(): east = lax.ppermute(tall[:, :halo], axes, westward)  3.84 us
    ppermute x2, starting transfers between devices, with_halo(): other = lax.ppermute(sent, 'slab', [(0, 2), (1, 3), (2, 0), (3, 1)])  2.16 us
  transfers between devices with their start and end apart: 6, of which 3 were waited for; matrix products, arithmetic and copies ran while one was open for 5% of the time, Pallas kernels for 48%

profile of v3, /device:TPU:24, one launch (start us, length us, event | category | flops | bytes accessed | tf_op | source)
XLA Modules:
  0.0 86.9 jit_solution(3713971672740661450)
XLA Ops:
  0.6 0.0 copy-start.4
  0.7 0.8 fusion.4
  1.5 0.9 %broadcast_multiply_fusion = bf16[3,128,256]{2,1,0:T(8,128)(2,1)S(1)} fusion(bf16[3,128,256]{2,1,0:T(8,128)(2,1)} %param.12, bf16[256]{0:T(256)(128)(2,1)S(1)} %fusion.4), kind=kLoop, calls=%fused_computation.20 | loop fusion | flops 98304 | bytes 393728 | tf_op jit(solution)/shard_map/mul | solution.py:302
  2.4 1.0 %pad_maximum_fusion.2 = bf16[6,128,256]{2,1,0:T(8,128)(2,1)S(1)} fusion(bf16[3,128,256]{2,1,0:T(8,128)(2,1)S(1)} %broadcast_multiply_fusion, bf16[3,128,256]{2,1,0:T(8,128)(2,1)} %param.11), kind=kLoop, calls=%fused_computation.5 | loop fusion | flops 196608 | bytes 786432 | tf_op jit(solution)/shard_map/concatenate | solution.py:302
  3.4 0.1 fusion.2
  3.5 1.6 %collective-permute-start.3 = (bf16[1,16,768]{1,2,0:T(8,128)(2,1)S(1)}, bf16[1,16,768]{1,2,0:T(8,128)(2,1)S(1)}, u32[]{:S(2)}, u32[]{:S(2)}) collective-permute-start(bf16[1,16,768]{1,2,0:T(8,128)(2,1)S(1)} %fusion.2), channel_id=1, source_target_pairs={{0,2},{1,3},{2,0},{3,1},{4,6},{5,7},{6,4},{7,5},{8,10},{9,11},{10,... | collective-permute-start | bytes 73736 | tf_op jit(solution)/shard_map/ppermute | solution.py:280
  5.1 0.7 convolution_convert_fusion
  5.8 0.1 fusion.5
  6.0 0.6 collective-permute-start
  6.5 0.2 copy.18
  6.7 4.6 %collective-permute-done.3 = bf16[1,16,768]{1,2,0:T(8,128)(2,1)S(1)} collective-permute-done((bf16[1,16,768]{1,2,0:T(8,128)(2,1)S(1)}, bf16[1,16,768]{1,2,0:T(8,128)(2,1)S(1)}, u32[]{:S(2)}, u32[]{:S(2)}) %collective-permute-start.3) | collective-permute-done | bytes 24608 | tf_op jit(solution)/shard_map/ppermute | solution.py:280
  11.3 0.1 copy.20
  11.4 0.1 copy.19
  11.5 0.1 pad_maximum_fusion.12
  11.7 1.9 %collective-permute-start.5 = (bf16[18,1,768]{2,1,0:T(2,128)(2,1)S(1)}, bf16[18,1,768]{2,1,0:T(2,128)(2,1)S(1)}, u32[]{:S(2)}, u32[]{:S(2)}) collective-permute-start(bf16[18,1,768]{2,1,0:T(2,128)(2,1)S(1)} %get-tuple-element.15), channel_id=1, source_target_pairs={{1,0},{3,2},{4,1},{6,3},{5,4},{7,6},{8,5},{10,7},{9,8},{11,10},{12... | collective-permute-start | bytes 82952 | tf_op jit(solution)/shard_map/ppermute | solution.py:293
  13.6 2.4 %collective-permute-start.4 = (bf16[18,1,768]{2,1,0:T(2,128)(2,1)S(1)}, bf16[18,1,768]{2,1,0:T(2,128)(2,1)S(1)}, u32[]{:S(2)}, u32[]{:S(2)}) collective-permute-start(bf16[18,1,768]{2,1,0:T(2,128)(2,1)S(1)} %get-tuple-element.14), channel_id=1, source_target_pairs={{0,1},{2,3},{1,4},{3,6},{4,5},{6,7},{5,8},{7,10},{8,9},{10,11},{9,... | collective-permute-start | bytes 82952 | tf_op jit(solution)/shard_map/ppermute | solution.py:292
  16.0 0.7 compare_convert_fusion.occupied
  16.7 3.3 %collective-permute-done.4 = bf16[18,1,768]{2,1,0:T(2,128)(2,1)S(1)} collective-permute-done((bf16[18,1,768]{2,1,0:T(2,128)(2,1)S(1)}, bf16[18,1,768]{2,1,0:T(2,128)(2,1)S(1)}, u32[]{:S(2)}, u32[]{:S(2)}) %collective-permute-start.4) | collective-permute-done | bytes 27680 | tf_op jit(solution)/shard_map/ppermute | solution.py:292
  20.0 0.3 pad_maximum_fusion.1
  20.3 0.6 reshape.54
  20.9 0.1 pad_bitcast_fusion.particle_ref
  21.0 41.6 %near.1 = f32[16,8,2048]{2,1,0:T(8,128)S(1)} custom-call(bf16[48,16]{1,0:T(8,128)(2,1)S(1)} %copy-done.2, bf16[18,8,2304]{2,1,0:T(8,128)(2,1)S(1)} %pad_bitcast_fusion.particle_ref), custom_call_target="tpu_custom_call" | custom-call | flops 40000000000 | bytes 2000000 | tf_op jit(solution)/shard_map/near/pallas_call | solution.py:258
  62.6 0.1 slice.61
  62.7 0.3 reshape.61
  63.0 0.2 pad_maximum_fusion.7
  63.2 1.9 %collective-permute-start.2 = (bf16[20,2,1536]{2,1,0:T(2,128)(2,1)S(1)}, bf16[20,2,1536]{2,1,0:T(2,128)(2,1)S(1)}, u32[]{:S(2)}, u32[]{:S(2)}) collective-permute-start(bf16[20,2,1536]{2,1,0:T(2,128)(2,1)S(1)} %get-tuple-element.7), channel_id=1, source_target_pairs={{1,0},{3,2},{4,1},{6,3},{5,4},{7,6},{8,5},{10,7},{9,8},{11,10},{12... | collective-permute-start | bytes 368648 | tf_op jit(solution)/shard_map/ppermute | solution.py:293
  65.2 2.4 %collective-permute-start.1 = (bf16[20,2,1536]{2,1,0:T(2,128)(2,1)S(1)}, bf16[20,2,1536]{2,1,0:T(2,128)(2,1)S(1)}, u32[]{:S(2)}, u32[]{:S(2)}) collective-permute-start(bf16[20,2,1536]{2,1,0:T(2,128)(2,1)S(1)} %get-tuple-element.6), channel_id=1, source_target_pairs={{0,1},{2,3},{1,4},{3,6},{4,5},{6,7},{5,8},{7,10},{8,9},{10,11},{9,... | collective-permute-start | bytes 368648 | tf_op jit(solution)/shard_map/ppermute | solution.py:292
  67.6 0.1 bitcast_multiply_fusion
  67.7 0.9 %copy.22 = f32[3,128,256]{2,1,0:T(8,128)} copy(f32[3,128,256]{1,2,0:T(8,128)S(1)} %bitcast_multiply_fusion) | data formatting | bytes 786432
  68.6 3.7 %collective-permute-done.1 = bf16[20,2,1536]{2,1,0:T(2,128)(2,1)S(1)} collective-permute-done((bf16[20,2,1536]{2,1,0:T(2,128)(2,1)S(1)}, bf16[20,2,1536]{2,1,0:T(2,128)(2,1)S(1)}, u32[]{:S(2)}, u32[]{:S(2)}) %collective-permute-start.1) | collective-permute-done | bytes 122912 | tf_op jit(solution)/shard_map/ppermute | solution.py:292
  72.3 0.8 pad_maximum_fusion.wide
  73.1 13.8 %far.1 = f32[3,488,256]{2,1,0:T(8,128)} custom-call(s32[108,3]{1,0:T(8,128)S(1)} %copy-done.1, bf16[20,20,1536]{2,1,0:T(8,128)(2,1)S(1)} %pad_maximum_fusion.wide, bf16[40,2,256,256]{3,2,1,0:T(8,128)(2,1)} %constant.36.clone.weights, bf16[488,1024]{1,0:T(8,128)(2,1)S(1)} %copy-done, f32[1,256]{1,0:T(1,128)S(1)} %compare_convert_fusion.occupied), custom_call_target="tpu_custom_call" | custom-call | tf_op jit(solution)/shard_map/far/pallas_call | solution.py:154
  (16 shorter events, 0.1 us)
Async XLA Ops:
  0.6 4.5 %copy-start.4 = (bf16[488,512,1]{1,0,2:T(8,128)(2,1)S(1)}, bf16[488,512,1]{1,0,2:T(8,128)(2,1)}, u32[]{:S(2)}) copy-start(bf16[488,512,1]{1,0,2:T(8,128)(2,1)} %constant.43) | copy-start | bytes 1499140
  0.6 4.5 %copy-start.3 = (bf16[3,488,256]{2,1,0:T(8,128)(2,1)S(1)}, bf16[3,488,256]{2,1,0:T(8,128)(2,1)}, u32[]{:S(2)}) copy-start(bf16[3,488,256]{2,1,0:T(8,128)(2,1)} %param.10) | copy-start | bytes 2248708
  3.5 7.8 %collective-permute-start.3 = (bf16[1,16,768]{1,2,0:T(8,128)(2,1)S(1)}, bf16[1,16,768]{1,2,0:T(8,128)(2,1)S(1)}, u32[]{:S(2)}, u32[]{:S(2)}) collective-permute-start(bf16[1,16,768]{1,2,0:T(8,128)(2,1)S(1)} %fusion.2), channel_id=1, source_target_pairs={{0,2},{1,3},{2,0},{3,1},{4,6},{5,7},{6,4},{7,5},{8,10},{9,11},{10,... | collective-permute-start | bytes 73736 | tf_op jit(solution)/shard_map/ppermute | solution.py:280
  6.0 57.0 %collective-permute-start = (bf16[2,16,1536]{2,1,0:T(8,128)(2,1)S(1)}, bf16[2,16,1536]{2,1,0:T(8,128)(2,1)S(1)}, u32[]{:S(2)}, u32[]{:S(2)}) collective-permute-start(bf16[2,16,1536]{2,1,0:T(8,128)(2,1)S(1)} %bitcast.38), channel_id=1, source_target_pairs={{0,2},{1,3},{2,0},{3,1},{4,6},{5,7},{6,4},{7,5},{8,10},{9,11},{10,... | collective-permute-start | bytes 294920 | tf_op jit(solution)/shard_map/ppermute | solution.py:280
  11.7 5.0 %collective-permute-start.5 = (bf16[18,1,768]{2,1,0:T(2,128)(2,1)S(1)}, bf16[18,1,768]{2,1,0:T(2,128)(2,1)S(1)}, u32[]{:S(2)}, u32[]{:S(2)}) collective-permute-start(bf16[18,1,768]{2,1,0:T(2,128)(2,1)S(1)} %get-tuple-element.15), channel_id=1, source_target_pairs={{1,0},{3,2},{4,1},{6,3},{5,4},{7,6},{8,5},{10,7},{9,8},{11,10},{12... | collective-permute-start | bytes 82952 | tf_op jit(solution)/shard_map/ppermute | solution.py:293
  13.6 6.4 %collective-permute-start.4 = (bf16[18,1,768]{2,1,0:T(2,128)(2,1)S(1)}, bf16[18,1,768]{2,1,0:T(2,128)(2,1)S(1)}, u32[]{:S(2)}, u32[]{:S(2)}) collective-permute-start(bf16[18,1,768]{2,1,0:T(2,128)(2,1)S(1)} %get-tuple-element.14), channel_id=1, source_target_pairs={{0,1},{2,3},{1,4},{3,6},{4,5},{6,7},{5,8},{7,10},{8,9},{10,11},{9,... | collective-permute-start | bytes 82952 | tf_op jit(solution)/shard_map/ppermute | solution.py:292
  20.3 0.7 copy-start.2
  63.2 5.4 %collective-permute-start.2 = (bf16[20,2,1536]{2,1,0:T(2,128)(2,1)S(1)}, bf16[20,2,1536]{2,1,0:T(2,128)(2,1)S(1)}, u32[]{:S(2)}, u32[]{:S(2)}) collective-permute-start(bf16[20,2,1536]{2,1,0:T(2,128)(2,1)S(1)} %get-tuple-element.7), channel_id=1, source_target_pairs={{1,0},{3,2},{4,1},{6,3},{5,4},{7,6},{8,5},{10,7},{9,8},{11,10},{12... | collective-permute-start | bytes 368648 | tf_op jit(solution)/shard_map/ppermute | solution.py:293
  65.2 7.1 %collective-permute-start.1 = (bf16[20,2,1536]{2,1,0:T(2,128)(2,1)S(1)}, bf16[20,2,1536]{2,1,0:T(2,128)(2,1)S(1)}, u32[]{:S(2)}, u32[]{:S(2)}) collective-permute-start(bf16[20,2,1536]{2,1,0:T(2,128)(2,1)S(1)} %get-tuple-element.6), channel_id=1, source_target_pairs={{0,1},{2,3},{1,4},{3,6},{4,5},{6,7},{5,8},{7,10},{8,9},{10,11},{9,... | collective-permute-start | bytes 368648 | tf_op jit(solution)/shard_map/ppermute | solution.py:292
  68.6 4.5 %copy-start = (bf16[488,1024]{1,0:T(8,128)(2,1)S(1)}, bf16[488,1024]{1,0:T(8,128)(2,1)}, u32[]{:S(2)}) copy-start(bf16[488,1024]{1,0:T(8,128)(2,1)} %constant.38.clone.unfold) | copy-start | bytes 2998276
  68.6 4.5 %copy-start.1 = (s32[108,3]{1,0:T(8,128)S(1)}, s32[108,3]{1,0:T(8,128)}, u32[]{:S(2)}) copy-start(s32[108,3]{1,0:T(8,128)} %constant.39.clone.steps) | copy-start | bytes 3892
